TPU v7x, 32 devices: a whole 2x2x4 slice. The times are simulated.
32 devices in a mesh: section: 2 (over x), dp: 8 (over z, core), tensor: 2 (over y).
Axes of the slice: x: 2, y: 2, z: 4, core: 2. Of those that a mesh axis runs over, the one named last changes fastest.
Arguments:
- ends_in: bfloat16 [2, 2, 2048, 2048], P('section', None, ('dp', 'tensor')), may hold values from -6 to 6
- pieces: int32 [2, 2], replicated, may hold values from 0 to 1792, as said below
- w_query: bfloat16 [2, 2048, 2048], P('section', 'dp', 'tensor'), may hold values from -0.125 to 0.125
- w_keyval: bfloat16 [2, 2048, 256], P('section', ('dp', 'tensor')), may hold values from -0.125 to 0.125
- w_output: bfloat16 [2, 2048, 2048], P('section', 'tensor', 'dp'), may hold values from -1.5 to 1.5
- w_hidden: bfloat16 [2, 2048, 8192], P('section', 'dp', 'tensor'), may hold values from -0.125 to 0.125
- w_project: bfloat16 [2, 8192, 2048], P('section', 'tensor', 'dp'), may hold values from -0.0625 to 0.0625
- norm_params: bfloat16 [2, 4, 2048], P('section', None, ('dp', 'tensor')), as said below
Outputs:
- ends_out: float32 [2, 2, 2048, 2048], P('section', None, ('dp', 'tensor'))
- grad_query: float32 [2, 2048, 2048], P('section', 'dp', 'tensor')
- grad_keyval: float32 [2, 2048, 256], P('section', ('dp', 'tensor'))
- grad_output: float32 [2, 2048, 2048], P('section', 'tensor', 'dp')
- grad_hidden: float32 [2, 2048, 8192], P('section', 'dp', 'tensor')
- grad_project: float32 [2, 8192, 2048], P('section', 'tensor', 'dp')
- grad_norms: float32 [2, 3, 2048], P('section', None, ('dp', 'tensor'))
- grad_shift: float32 [2, 2048], P('section', ('dp', 'tensor'))
Inputs may be any that keep to these rules, and one draw needn't show every extreme that they name: Each sequence has 2 picture pieces of 256 positions; the j-th starts between j * (1024) and (j + 1) * 1024 - 256. `norm_params`: gains in rows 0 and 2 lie between 0.5 and 1.5.
All inputs are finite; a program needn't handle non-finite values.
Results may differ from a plain program's by a relative error of at most 0.02.
Values may be sent and summed in bfloat16 or wider, within the bound.
No kernel may reach another device: no remote copies, remote signals or barrier semaphores. Data moves between devices by JAX's collectives and lax.ppermute only.
A program may use at most 384 MiB of HBM per device.

v0:
```python
import jax
import jax.numpy as jnp
from jax import lax
from jax.sharding import PartitionSpec as P

SPAN = 256
MICRO = 2
EPSILON = 1e-05
NEGATIVE = -1000000000.0


def in_blocks(array, dim, devices):
    shape = array.shape
    blocks = array.reshape(*shape[:dim], devices, shape[dim] // devices, *shape[dim + 1 :])
    return jnp.moveaxis(blocks, dim, 0)


def sum_at_owner(array, axis, dim):
    devices = lax.axis_size(axis)
    blocks = lax.all_to_all(in_blocks(array, dim, devices), axis, 0, 0, tiled=True)
    return jnp.sum(blocks.astype(jnp.float32), axis=0)


def from_behind(block, axis, distance):
    devices = range(lax.axis_size(axis))
    route = [(i - distance, i) for i in devices if i - distance in devices]
    return lax.ppermute(block, axis, route)


def layer_norm(values, scale_row, shift_row):
    centered = values - jnp.mean(values, -1, keepdims=True)
    spread = jnp.mean(centered * centered, -1, keepdims=True)
    return centered * lax.rsqrt(spread + EPSILON) * scale_row + shift_row


def gelu_tanh(values):
    return jax.nn.gelu(values, approximate=True)


def spread_rows(values):
    return lax.all_gather(values, "tensor", axis=1, tiled=True)


def collect_rows(terms):
    return lax.psum_scatter(
        terms.astype(jnp.bfloat16), "tensor", scatter_dimension=1, tiled=True
    ).astype(jnp.float32)


def spread_grads(values):
    return lax.all_gather(values, "tensor", axis=1, tiled=True)


def collect_grads(terms):
    return lax.psum_scatter(
        terms.astype(jnp.bfloat16), "tensor", scatter_dimension=1, tiled=True
    ).astype(jnp.float32)


def allowed_keys(starts, query_start, query_rows, length):
    query_pos = query_start + jnp.arange(query_rows, dtype=jnp.int32)
    key_pos = jnp.arange(length, dtype=jnp.int32)
    causal = key_pos[None, :] <= query_pos[:, None]
    query_in = (query_pos[None, None, :] >= starts[:, :, None]) & (
        query_pos[None, None, :] < starts[:, :, None] + SPAN
    )
    key_in = (key_pos[None, None, :] >= starts[:, :, None]) & (
        key_pos[None, None, :] < starts[:, :, None] + SPAN
    )
    shared_piece = jnp.any(query_in[:, :, :, None] & key_in[:, :, None, :], axis=1)
    return causal[None] | shared_piece


def scores_of(queries, keyval_all, allowed):
    head_size = keyval_all.shape[-1] // 2
    queries_four = queries.reshape(queries.shape[0], queries.shape[1], -1, head_size)
    keys_part = keyval_all[..., :head_size]
    scores = jnp.einsum(
        "sqhd,skd->shqk", queries_four, keys_part, preferred_element_type=jnp.float32
    ) * head_size ** (-0.5)
    return (jnp.where(allowed[:, None], scores, NEGATIVE), queries_four)


def attend_forward(queries, keyval_all, allowed):
    head_size = keyval_all.shape[-1] // 2
    scores, queries_four = scores_of(queries, keyval_all, allowed)
    peak = jnp.max(scores, -1, keepdims=True)
    log_total = peak + jnp.log(jnp.sum(jnp.exp(scores - peak), -1, keepdims=True))
    probs = jnp.exp(scores - log_total).astype(jnp.bfloat16)
    values_part = keyval_all[..., head_size:]
    attended = jnp.einsum(
        "shqk,skd->sqhd", probs, values_part, preferred_element_type=jnp.float32
    ).astype(jnp.bfloat16)
    return (log_total, attended.reshape(queries.shape))


def attend_backward(queries, keyval_all, log_total, grad_attended, allowed):
    head_size = keyval_all.shape[-1] // 2
    scores, queries_four = scores_of(queries, keyval_all, allowed)
    probs = jnp.exp(scores - log_total)
    keys_part = keyval_all[..., :head_size]
    values_part = keyval_all[..., head_size:]
    grad_four = grad_attended.reshape(queries_four.shape)
    grad_probs = jnp.einsum(
        "sqhd,skd->shqk", grad_four, values_part, preferred_element_type=jnp.float32
    )
    grad_values = jnp.einsum(
        "shqk,sqhd->skd", probs.astype(jnp.bfloat16), grad_four, preferred_element_type=jnp.float32
    )
    weighted = jnp.sum(probs * grad_probs, -1, keepdims=True)
    grad_scores = (probs * (grad_probs - weighted) * head_size ** (-0.5)).astype(jnp.bfloat16)
    grad_queries = jnp.einsum(
        "shqk,skd->sqhd", grad_scores, keys_part, preferred_element_type=jnp.float32
    )
    grad_queries = grad_queries.astype(jnp.bfloat16).reshape(queries.shape)
    grad_keys = jnp.einsum(
        "shqk,sqhd->skd", grad_scores, queries_four, preferred_element_type=jnp.float32
    )
    return (grad_queries, jnp.concatenate([grad_keys, grad_values], -1))


def layer_forward(inputs, weights, allowed):
    query_mat, keyval_mat, output_mat, hidden_mat, project_mat, norm_table = weights
    normed_local = layer_norm(inputs, norm_table[0], norm_table[1]).astype(jnp.bfloat16)
    keyval_local = jnp.einsum(
        "srd,de->sre", normed_local, keyval_mat, preferred_element_type=jnp.float32
    ).astype(jnp.bfloat16)
    keyval_all = lax.all_gather(keyval_local, ("dp", "tensor"), axis=1, tiled=True)
    normed_rows = spread_rows(normed_local)
    queries = jnp.einsum(
        "sqd,de->sqe", normed_rows, query_mat, preferred_element_type=jnp.float32
    ).astype(jnp.bfloat16)
    log_total, attended = attend_forward(queries, keyval_all, allowed)
    middle = inputs + collect_rows(
        jnp.einsum("sqe,ed->sqd", attended, output_mat, preferred_element_type=jnp.float32)
    )
    mixed_local = layer_norm(middle, norm_table[2], norm_table[3]).astype(jnp.bfloat16)
    mixed_rows = spread_rows(mixed_local)
    hidden_pre = jnp.einsum(
        "sqd,df->sqf", mixed_rows, hidden_mat, preferred_element_type=jnp.float32
    )
    hidden_act = gelu_tanh(hidden_pre).astype(jnp.bfloat16)
    outputs = middle + collect_rows(
        jnp.einsum("sqf,fd->sqd", hidden_act, project_mat, preferred_element_type=jnp.float32)
    )
    saved = (
        normed_local,
        normed_rows,
        keyval_all,
        queries,
        log_total,
        attended,
        middle,
        mixed_rows,
        hidden_pre,
        hidden_act,
    )
    return (outputs, saved)


def input_backward(inputs, grad_out, weights, allowed, saved):
    query_mat, keyval_mat, output_mat, hidden_mat, project_mat, norm_table = weights
    (
        normed_local,
        normed_rows,
        keyval_all,
        queries,
        log_total,
        attended,
        middle,
        mixed_rows,
        hidden_pre,
        hidden_act,
    ) = saved
    grad_branch = spread_grads(grad_out.astype(jnp.bfloat16))
    grad_act = jnp.einsum(
        "sqd,fd->sqf", grad_branch, project_mat, preferred_element_type=jnp.float32
    )
    grad_pre = jax.vjp(gelu_tanh, hidden_pre)[1](grad_act)[0].astype(jnp.bfloat16)
    grad_mixed = collect_grads(
        jnp.einsum("sqf,df->sqd", grad_pre, hidden_mat, preferred_element_type=jnp.float32)
    )
    second_pull = jax.vjp(layer_norm, middle, norm_table[2], norm_table[3])[1]
    grad_mid_norm, grad_gain_two, grad_bias_two = second_pull(grad_mixed)
    grad_middle = grad_out + grad_mid_norm
    grad_attn_rows = spread_grads(grad_middle.astype(jnp.bfloat16))
    grad_attended = jnp.einsum(
        "sqd,ed->sqe", grad_attn_rows, output_mat, preferred_element_type=jnp.float32
    ).astype(jnp.bfloat16)
    grad_queries, keyval_terms = attend_backward(
        queries, keyval_all, log_total, grad_attended, allowed
    )
    grad_keyval = sum_at_owner(keyval_terms.astype(jnp.bfloat16), ("dp", "tensor"), 1).astype(
        jnp.bfloat16
    )
    grad_normed = collect_grads(
        jnp.einsum("sqe,de->sqd", grad_queries, query_mat, preferred_element_type=jnp.float32)
    )
    grad_normed = grad_normed + jnp.einsum(
        "sre,de->srd", grad_keyval, keyval_mat, preferred_element_type=jnp.float32
    )
    first_pull = jax.vjp(layer_norm, inputs, norm_table[0], norm_table[1])[1]
    grad_in_norm, grad_gain_one, grad_bias_one = first_pull(grad_normed)
    grad_inputs = grad_middle + grad_in_norm
    grad_table = jnp.stack([grad_gain_one, grad_bias_one, grad_gain_two, grad_bias_two])
    pairs = (
        (normed_rows, grad_queries),
        (attended, grad_attn_rows),
        (mixed_rows, grad_pre),
        (hidden_act, grad_branch),
        (normed_local, grad_keyval),
    )
    return (grad_inputs, grad_table, pairs)


def weight_products(pairs):
    grad_querymat = jnp.einsum(
        "sqd,sqe->de", pairs[0][0], pairs[0][1], preferred_element_type=jnp.float32
    )
    grad_outmat = jnp.einsum(
        "sqe,sqd->ed", pairs[1][0], pairs[1][1], preferred_element_type=jnp.float32
    )
    grad_hidmat = jnp.einsum(
        "sqd,sqf->df", pairs[2][0], pairs[2][1], preferred_element_type=jnp.float32
    )
    grad_projmat = jnp.einsum(
        "sqf,sqd->fd", pairs[3][0], pairs[3][1], preferred_element_type=jnp.float32
    )
    grad_keyvalmat = jnp.einsum(
        "srd,sre->de", pairs[4][0], pairs[4][1], preferred_element_type=jnp.float32
    )
    return (grad_querymat, grad_outmat, grad_hidmat, grad_projmat, grad_keyvalmat)


def local(ends_in, pieces, w_query, w_keyval, w_output, w_hidden, w_project, norm_params):
    section_index = lax.axis_index("section")
    per_batch = ends_in.shape[1] // MICRO
    rows_local = ends_in.shape[2]
    width = ends_in.shape[3]
    local_ends = ends_in[0].reshape(MICRO, per_batch, rows_local, width)
    starts_all = pieces.reshape(MICRO, per_batch, pieces.shape[1])
    gathered = (
        lax.all_gather(w_query, "dp", axis=1, tiled=True),
        lax.all_gather(w_output, "dp", axis=2, tiled=True),
        lax.all_gather(w_hidden, "dp", axis=1, tiled=True),
        lax.all_gather(w_project, "dp", axis=2, tiled=True),
    )
    shared = (
        lax.all_gather(w_keyval, ("dp", "tensor"), axis=1, tiled=True),
        lax.all_gather(norm_params, ("dp", "tensor"), axis=2, tiled=True),
    )
    weights = (
        gathered[0][0],
        shared[0][0],
        gathered[1][0],
        gathered[2][0],
        gathered[3][0],
        shared[1][0].astype(jnp.float32),
    )
    query_rows = rows_local * lax.axis_size("tensor")
    query_start = lax.axis_index("dp") * query_rows
    length = query_rows * lax.axis_size("dp")
    incoming = jnp.zeros((per_batch, rows_local, width), jnp.bfloat16)
    stored = []
    layer_outs = []
    saved_list = []
    for tick_now in range(MICRO + 1):
        batch_clip = jnp.clip(tick_now - section_index, 0, MICRO - 1)
        starts = lax.dynamic_index_in_dim(starts_all, batch_clip, 0, keepdims=False)
        allowed = allowed_keys(starts, query_start, query_rows, length)
        own_rows = local_ends[min(tick_now, MICRO - 1)]
        inputs_now = jnp.where(section_index == 0, own_rows, incoming)
        stored.append(inputs_now)
        outputs, saved_now = layer_forward(inputs_now.astype(jnp.float32), weights, allowed)
        layer_outs.append(outputs)
        saved_list.append(saved_now)
        if tick_now < MICRO:
            incoming = from_behind(outputs.astype(jnp.bfloat16), "section", 1)
    stored_stack = jnp.stack(stored)
    saved_stack = tuple((jnp.stack(items) for items in zip(*saved_list)))
    totals = tuple(
        (
            jnp.zeros((1,) + arr.shape, jnp.float32)
            for arr in (weights[0], weights[2], weights[3], weights[4], weights[1])
        )
    )
    table_total = jnp.zeros((1,) + weights[5].shape, jnp.float32)
    received = jnp.zeros((per_batch, rows_local, width), jnp.bfloat16)
    input_grads = []
    for tick_now in range(MICRO + 1):
        batch_index = tick_now - 1 + section_index
        valid = ((batch_index >= 0) & (batch_index < MICRO)).astype(jnp.float32)
        batch_clip = jnp.clip(batch_index, 0, MICRO - 1)
        source_tick = jnp.clip(tick_now - 1 + 2 * section_index, 0, MICRO)
        inputs_now = lax.dynamic_index_in_dim(stored_stack, source_tick, 0, keepdims=False).astype(
            jnp.float32
        )
        starts = lax.dynamic_index_in_dim(starts_all, batch_clip, 0, keepdims=False)
        allowed = allowed_keys(starts, query_start, query_rows, length)
        fed_back = local_ends[min(tick_now, MICRO - 1)]
        grad_now = jnp.where(section_index == 1, fed_back, received).astype(jnp.float32)
        saved_now = tuple(
            (lax.dynamic_index_in_dim(item, source_tick, 0, keepdims=False) for item in saved_stack)
        )
        grad_inputs, grad_table, pairs = input_backward(
            inputs_now, grad_now, weights, allowed, saved_now
        )
        input_grads.append(grad_inputs)
        table_total = table_total + grad_table[None] * valid
        if tick_now < MICRO:
            received = from_behind(grad_inputs.astype(jnp.bfloat16), "section", -1)
        products = weight_products(pairs)
        totals = tuple((total + term[None] * valid for total, term in zip(totals, products)))
    large_part = (
        lax.psum_scatter(
            totals[0].astype(jnp.bfloat16), "dp", scatter_dimension=1, tiled=True
        ).astype(jnp.float32),
        lax.psum_scatter(
            totals[1].astype(jnp.bfloat16), "dp", scatter_dimension=2, tiled=True
        ).astype(jnp.float32),
        lax.psum_scatter(
            totals[2].astype(jnp.bfloat16), "dp", scatter_dimension=1, tiled=True
        ).astype(jnp.float32),
        lax.psum_scatter(
            totals[3].astype(jnp.bfloat16), "dp", scatter_dimension=2, tiled=True
        ).astype(jnp.float32),
    )
    small_part = (
        lax.psum_scatter(totals[4], ("dp", "tensor"), scatter_dimension=1, tiled=True),
        lax.psum_scatter(table_total, ("dp", "tensor"), scatter_dimension=2, tiled=True),
    )
    norm_totals = small_part[1]
    result_rows = [
        jnp.where(section_index == 0, input_grads[index + 1], layer_outs[index + 1])
        for index in range(MICRO)
    ]
    ends_out = jnp.stack(result_rows).reshape(1, MICRO * per_batch, rows_local, width)
    return (
        ends_out,
        large_part[0],
        small_part[0],
        large_part[1],
        large_part[2],
        large_part[3],
        norm_totals[:, :3],
        norm_totals[:, 3],
    )


def solution(mesh):
    placed = (
        P("section", None, ("dp", "tensor"), None),
        P(),
        P("section", "dp", "tensor"),
        P("section", ("dp", "tensor"), None),
        P("section", "tensor", "dp"),
        P("section", "dp", "tensor"),
        P("section", "tensor", "dp"),
        P("section", None, ("dp", "tensor")),
    )
    return jax.shard_map(
        local,
        mesh=mesh,
        in_specs=placed,
        out_specs=(
            P("section", None, ("dp", "tensor"), None),
            P("section", "dp", "tensor"),
            P("section", ("dp", "tensor"), None),
            P("section", "tensor", "dp"),
            P("section", "dp", "tensor"),
            P("section", "tensor", "dp"),
            P("section", None, ("dp", "tensor")),
            P("section", ("dp", "tensor")),
        ),
        check_vma=False,
    )
```

profile of v0, /device:TPU:0, one launch (start us, length us, event | category | flops | bytes accessed | tf_op | source)
XLA Modules:
  0.0 2126.1 jit_solution(3505118352944656290)
XLA Ops:
  8.0 34.1 %all_gather.65 = bf16[1,4,2048]{2,1,0:T(4,128)(2,1)S(1)} all-gather(bf16[1,4,128]{2,1,0:T(4,128)(2,1)} %param.15), channel_id=1, replica_groups=mesh['section'=2,'dp'=8,'tensor'=2] {'dp','tensor'}, dimensions={2}, use_global_device_ids=true | all-gather | bytes 17408 | tf_op jit(solution)/shard_map/all_gather | solution.py:250
  73.4 48.8 %all-gather.31.cloned.1.call-done = bf16[1,2048,1024]{2,1,0:T(8,128)(2,1)} async-done(((bf16[1,256,1024]{2,1,0:T(8,128)(2,1)}), bf16[1,2048,1024]{2,1,0:T(8,128)(2,1)}) %all-gather.31.cloned.1.call-update) | async-done | bytes 4194320 | tf_op jit(solution)/shard_map/all_gather | solution.py:243
  125.9 35.6 %all-gather.59.cloned.1.call-done = bf16[2048,256]{1,0:T(8,128)(2,1)} async-done(((bf16[128,256]{1,0:T(8,128)(2,1)}), bf16[2048,256]{1,0:T(8,128)(2,1)}) %all-gather.59.cloned.1.call-update) | async-done | bytes 1048592 | tf_op jit(solution)/shard_map/all_gather | solution.py:128
  187.7 22.0 %all-gather.33.cloned.1.call-done = bf16[1,1024,2048]{2,1,0:T(8,128)(2,1)} async-done(((bf16[1,1024,256]{2,1,0:T(8,128)(2,1)}), bf16[1,1024,2048]{2,1,0:T(8,128)(2,1)}) %all-gather.33.cloned.1.call-update) | async-done | bytes 4194320 | tf_op jit(solution)/shard_map/all_gather | solution.py:244
  214.2 18.7 reduce-scatter.21.cloned.1.call-done
  240.3 19.7 all-gather.35.cloned.1.call-done
  260.0 152.8 %all-gather.37.cloned.1.call-done = bf16[1,2048,4096]{2,1,0:T(8,128)(2,1)} async-done(((bf16[1,256,4096]{2,1,0:T(8,128)(2,1)}), bf16[1,2048,4096]{2,1,0:T(8,128)(2,1)}) %all-gather.37.cloned.1.call-update) | async-done | bytes 16777232 | tf_op jit(solution)/shard_map/all_gather | solution.py:245
  425.4 139.2 %all-gather.25.cloned.1.call-done = bf16[1,4096,2048]{2,1,0:T(8,128)(2,1)} async-done(((bf16[1,4096,256]{2,1,0:T(8,128)(2,1)}), bf16[1,4096,2048]{2,1,0:T(8,128)(2,1)}) %all-gather.25.cloned.1.call-update) | async-done | bytes 16777232 | tf_op jit(solution)/shard_map/all_gather | solution.py:246
  640.8 36.1 %all-gather.61.cloned.1.call-done = bf16[2048,256]{1,0:T(8,128)(2,1)} async-done(((bf16[128,256]{1,0:T(8,128)(2,1)}), bf16[2048,256]{1,0:T(8,128)(2,1)}) %all-gather.61.cloned.1.call-update) | async-done | bytes 1048592 | tf_op jit(solution)/shard_map/all_gather | solution.py:128
  709.3 19.2 reduce-scatter.25.cloned.1.call-done
  734.2 21.4 %all-gather.41.cloned.1.call-done = bf16[1,256,2048]{2,1,0:T(8,128)(2,1)} async-done(((bf16[1,128,2048]{2,1,0:T(8,128)(2,1)}), bf16[1,256,2048]{2,1,0:T(8,128)(2,1)}) %all-gather.41.cloned.1.call-update) | async-done | bytes 1048592 | tf_op jit(solution)/shard_map/all_gather | solution.py:41
  777.8 20.4 reduce-scatter.27.cloned.1.call-done
  842.1 36.9 %all-gather.63.cloned.1.call-done = bf16[2048,256]{1,0:T(8,128)(2,1)} async-done(((bf16[128,256]{1,0:T(8,128)(2,1)}), bf16[2048,256]{1,0:T(8,128)(2,1)}) %all-gather.63.cloned.1.call-update) | async-done | bytes 1048592 | tf_op jit(solution)/shard_map/all_gather | solution.py:128
  909.1 19.3 reduce-scatter.29.cloned.1.call-done
  935.6 20.1 all-gather.45.cloned.1.call-done
  1158.9 20.8 all-gather.49.cloned.1.call-done
  1204.2 20.6 reduce-scatter.35.cloned.1.call-done
  1311.8 19.1 all-to-all-done.1
  1361.3 20.7 all-gather.53.cloned.1.call-done
  1607.5 30.4 %fusion.1 = bf16[1,4096,2048]{2,1,0:T(8,128)(2,1)} fusion(f32[4096,2048]{1,0:T(8,128)} %fusion.230, f32[4096,2048]{1,0:T(8,128)} %fusion.232, f32[]{:T(128)S(6)} %convert_element_type.649, f32[]{:T(128)S(6)} %convert_element_type.648, f32[]{:T(128)S(6)} %convert_element_type.647, bf16[3,1,256,4096]{3,2,1,0:T(8,128)(2,1)} %copy-done.12, s32[]{:T(128)S(6)} %min.35, ...), kind=kOutput, calls=%fused_computation.3 | convolution fusion | flops 4345298944 | bytes 87031824 | tf_op jit(solution)/shard_map/sqf,sqd->fd/dot_general | solution.py:226
  1667.6 30.1 %fusion = bf16[1,2048,4096]{2,1,0:T(8,128)(2,1)} fusion(f32[2048,4096]{1,0:T(8,128)} %fusion.355, f32[2048,4096]{1,0:T(8,128)} %fusion.357, f32[]{:T(128)S(6)} %convert_element_type.649, f32[]{:T(128)S(6)} %convert_element_type.648, f32[]{:T(128)S(6)} %convert_element_type.647, bf16[256,4096]{1,0:T(8,128)(2,1)} %fusion.88, ...), kind=kOutput, calls=%fused_computation.2 | convolution fusion | flops 4345298944 | bytes 87031824 | tf_op jit(solution)/shard_map/sqd,sqf->df/dot_general | solution.py:223
  1719.1 166.6 %reduce-scatter.53.cloned.1.call-done = bf16[1,4096,256]{2,1,0:T(8,128)(2,1)} async-done(((bf16[1,4096,2048]{2,1,0:T(8,128)(2,1)}), bf16[1,4096,256]{2,1,0:T(8,128)(2,1)}) %reduce-scatter.53.cloned.1.call-update) | async-done | bytes 2097168 | tf_op jit(solution)/shard_map/reduce_scatter | solution.py:324
  1889.6 165.0 %reduce-scatter.51.cloned.1.call-done = bf16[1,256,4096]{2,1,0:T(8,128)(2,1)} async-done(((bf16[1,2048,4096]{2,1,0:T(8,128)(2,1)}), bf16[1,256,4096]{2,1,0:T(8,128)(2,1)}) %reduce-scatter.51.cloned.1.call-update) | async-done | bytes 2097168 | tf_op jit(solution)/shard_map/reduce_scatter | solution.py:321
  2058.8 60.7 %reduce-scatter.47.cloned.1.call-done = f32[1,128,256]{2,1,0:T(8,128)} async-done(((f32[1,2048,256]{2,1,0:T(8,128)}), f32[1,128,256]{2,1,0:T(8,128)}) %reduce-scatter.47.cloned.1.call-update) | async-done | bytes 131088 | tf_op jit(solution)/shard_map/reduce_scatter | solution.py:329
  (623 shorter events, 931.2 us)
Async XLA Ops:
  7.9 65.4 %all-gather.29.cloned.1.call-start = ((), (), s32[]{:S(2)}) async-start(), calls=%async_computation.23 | async-start | bytes 1572864 | tf_op jit(solution)/shard_map/all_gather | solution.py:41
  44.9 77.2 %all-gather.31.cloned.1.call-start = ((), (), s32[]{:S(2)}) async-start(), calls=%async_computation.24 | async-start | bytes 4718592 | tf_op jit(solution)/shard_map/all_gather | solution.py:243
  45.7 115.9 %all-gather.59.cloned.1.call-start = ((), (), s32[]{:S(2)}) async-start(), calls=%async_computation.55 | async-start | bytes 1114112 | tf_op jit(solution)/shard_map/all_gather | solution.py:128
  53.1 156.6 %all-gather.33.cloned.1.call-start = ((), (), s32[]{:S(2)}) async-start(), calls=%async_computation.25 | async-start | bytes 4718592 | tf_op jit(solution)/shard_map/all_gather | solution.py:244
  53.7 179.1 %reduce-scatter.21.cloned.1.call-start = ((), (), s32[]{:S(2)}) async-start(), calls=%async_computation.26 | async-start | bytes 1572864 | tf_op jit(solution)/shard_map/reduce_scatter | solution.py:45
  238.5 174.3 %all-gather.37.cloned.1.call-start = ((), (), s32[]{:S(2)}) async-start(), calls=%async_computation.28 | async-start | bytes 18874368 | tf_op jit(solution)/shard_map/all_gather | solution.py:245
  239.3 325.3 %all-gather.25.cloned.1.call-start = ((), (), s32[]{:S(2)}) async-start(), calls=%async_computation.21 | async-start | bytes 18874368 | tf_op jit(solution)/shard_map/all_gather | solution.py:246
  240.0 356.1 %reduce-scatter.23.cloned.1.call-start = ((), (), s32[]{:S(2)}) async-start(), calls=%async_computation.29 | async-start | bytes 1572864 | tf_op jit(solution)/shard_map/reduce_scatter | solution.py:45
  615.8 112.7 %reduce-scatter.25.cloned.1.call-start = ((), (), s32[]{:S(2)}) async-start(), calls=%async_computation.31 | async-start | bytes 1572864 | tf_op jit(solution)/shard_map/reduce_scatter | solution.py:45
  734.1 64.0 %reduce-scatter.27.cloned.1.call-start = ((), (), s32[]{:S(2)}) async-start(), calls=%async_computation.33 | async-start | bytes 1572864 | tf_op jit(solution)/shard_map/reduce_scatter | solution.py:45
  817.9 110.6 %reduce-scatter.29.cloned.1.call-start = ((), (), s32[]{:S(2)}) async-start(), calls=%async_computation.35 | async-start | bytes 1572864 | tf_op jit(solution)/shard_map/reduce_scatter | solution.py:45
  935.1 87.8 %reduce-scatter.31.cloned.1.call-start = ((), (), s32[]{:S(2)}) async-start(), calls=%async_computation.37 | async-start | bytes 1572864 | tf_op jit(solution)/shard_map/reduce_scatter | solution.py:55
  1110.1 69.6 %all-gather.49.cloned.1.call-start = ((), (), s32[]{:S(2)}) async-start(), calls=%async_computation.40 | async-start | bytes 1572864 | tf_op jit(solution)/shard_map/all_gather | solution.py:51
  1158.9 65.9 %reduce-scatter.35.cloned.1.call-start = ((), (), s32[]{:S(2)}) async-start(), calls=%async_computation.41 | async-start | bytes 1572864 | tf_op jit(solution)/shard_map/reduce_scatter | solution.py:55
  1311.7 70.3 %all-gather.53.cloned.1.call-start = ((), (), s32[]{:S(2)}) async-start(), calls=%async_computation.44 | async-start | bytes 1572864 | tf_op jit(solution)/shard_map/all_gather | solution.py:51
  1361.2 65.7 %reduce-scatter.39.cloned.1.call-start = ((), (), s32[]{:S(2)}) async-start(), calls=%async_computation.45 | async-start | bytes 1572864 | tf_op jit(solution)/shard_map/reduce_scatter | solution.py:55
  1432.5 109.3 %reduce-scatter.41.cloned.1.call-start = ((), (), s32[]{:S(2)}) async-start(), calls=%async_computation.47 | async-start | bytes 1572864 | tf_op jit(solution)/shard_map/reduce_scatter | solution.py:55
  1516.6 186.1 %reduce-scatter.43.cloned.1.call-start = ((), (), s32[]{:S(2)}) async-start(), calls=%async_computation.48 | async-start | bytes 1572864 | tf_op jit(solution)/shard_map/reduce_scatter | solution.py:45
  1529.9 176.7 %reduce-scatter.55.cloned.1.call-start = ((), (), s32[]{:S(2)}) async-start(), calls=%async_computation.58 | async-start | bytes 1114112
  1554.1 154.8 %reduce-scatter.49.cloned.1.call-start = ((), (), s32[]{:S(2)}) async-start(), calls=%async_computation.51 | async-start | bytes 4718592 | tf_op jit(solution)/shard_map/reduce_scatter | solution.py:318
  1563.3 153.7 %reduce-scatter.45.cloned.1.call-start = ((), (), s32[]{:S(2)}) async-start(), calls=%async_computation.49 | async-start | bytes 4718592 | tf_op jit(solution)/shard_map/reduce_scatter | solution.py:315
  1574.8 310.9 %reduce-scatter.53.cloned.1.call-start = ((), (), s32[]{:S(2)}) async-start(), calls=%async_computation.53 | async-start | bytes 18874368 | tf_op jit(solution)/shard_map/reduce_scatter | solution.py:324
  1637.9 416.7 %reduce-scatter.51.cloned.1.call-start = ((), (), s32[]{:S(2)}) async-start(), calls=%async_computation.52 | async-start | bytes 18874368 | tf_op jit(solution)/shard_map/reduce_scatter | solution.py:321
  1697.8 421.6 %reduce-scatter.47.cloned.1.call-start = ((), (), s32[]{:S(2)}) async-start(), calls=%async_computation.50 | async-start | bytes 2228224 | tf_op jit(solution)/shard_map/reduce_scatter | solution.py:329
  (171 other events, 6035.1 us)
Sparse Core Ops, SparseCore 0:
  10.2 40.6 all-gather.26
  75.0 47.1 all-gather.30
  124.8 36.6 all-gather.58
  162.9 46.7 all-gather.32
  261.6 151.0 all-gather.36
  414.5 150.0 all-gather.24
  613.9 22.3 all-gather.38
  638.9 37.9 all-gather.60
  734.3 21.3 all-gather.40
  815.9 22.3 all-gather.42
  840.9 37.9 all-gather.62
  934.3 21.2 all-gather.44
  957.1 21.2 all-gather.56
  1110.2 27.5 reduce-scatter.32
  1230.7 21.2 all-gather.50
  1311.8 27.5 reduce-scatter.36
  1432.7 21.3 all-gather.54
  1530.0 23.4 reduce-scatter.42
  1557.0 57.3 reduce-scatter.54
  1616.8 48.9 reduce-scatter.48
  1668.8 48.1 reduce-scatter.44
  1719.3 166.3 reduce-scatter.52
  1888.0 166.6 reduce-scatter.50
  2059.4 59.9 reduce-scatter.46
  (14 shorter events, 280.7 us)
where the time goes:
time: 2130 us
  waiting for transfers between devices  1310 us (62%)
  matrix products  516 us (24%)
  other arithmetic  180 us (8%)
  local copies, waits for them, and re-layouts  46.4 us (2%)
  blocking collectives  34.1 us (2%)
  starting transfers between devices  27.5 us (1%)
    reduce_scatter x1, waiting for transfers between devices, local(): lax.psum_scatter(totals[3].astype(jnp.bfloat16), 'dp', scatter_dimension=...  167 us
    reduce_scatter x1, waiting for transfers between devices, local(): lax.psum_scatter(totals[2].astype(jnp.bfloat16), 'dp', scatter_dimension=...  165 us
    all_gather x1, waiting for transfers between devices, local(): lax.all_gather(w_hidden, 'dp', axis=1, tiled=True)  153 us
    all_gather x1, waiting for transfers between devices, local(): lax.all_gather(w_project, 'dp', axis=2, tiled=True)  139 us
    all_gather x6, waiting for transfers between devices, spread_rows(): return lax.all_gather(values, 'tensor', axis=1, tiled=True)  110 us
    all_gather x3, waiting for transfers between devices, layer_forward(): lax.all_gather(keyval_local, ('dp', 'tensor'), axis=1, tiled=True)  109 us
    reduce_scatter x6, waiting for transfers between devices, collect_rows(): lax.psum_scatter(terms.astype(jnp.bfloat16), 'tensor', scatter_dimension=...  96.2 us
    all_gather x6, waiting for transfers between devices, spread_grads(): return lax.all_gather(values, 'tensor', axis=1, tiled=True)  69.8 us
  transfers between devices with their start and end apart: 45, of which 41 were waited for; matrix products, arithmetic and copies ran while one was open for 17% of the time, Pallas kernels for 0%

commit v1 on v0

--- a/solution.py
+++ b/solution.py
@@ -7,6 +7,29 @@
 MICRO = 2
 EPSILON = 1e-05
 NEGATIVE = -1000000000.0
+
+
+def laid_out(tiles, dim):
+    lengths = list(tiles.shape[1:])
+    lengths[dim] *= tiles.shape[0]
+    return jnp.moveaxis(tiles, 0, dim).reshape(lengths)
+
+
+def grow_blocks(x, axis):
+    size, here = (lax.axis_size(axis), lax.axis_index(axis))
+    blocks, bit = (x[None], 1)
+    while bit < size:
+        partner_block = lax.ppermute(blocks, axis, [(i, i ^ bit) for i in range(size)])
+        low = here & bit == 0
+        blocks = jnp.concatenate(
+            [jnp.where(low, blocks, partner_block), jnp.where(low, partner_block, blocks)]
+        )
+        bit *= 2
+    return blocks
+
+
+def collect(x, axis, dim):
+    return laid_out(grow_blocks(x, axis), dim)
 
 
 def in_blocks(array, dim, devices):
@@ -125,7 +148,7 @@
     keyval_local = jnp.einsum(
         "srd,de->sre", normed_local, keyval_mat, preferred_element_type=jnp.float32
     ).astype(jnp.bfloat16)
-    keyval_all = lax.all_gather(keyval_local, ("dp", "tensor"), axis=1, tiled=True)
+    keyval_all = collect(keyval_local, ("dp", "tensor"), 1)
     normed_rows = spread_rows(normed_local)
     queries = jnp.einsum(
         "sqd,de->sqe", normed_rows, query_mat, preferred_element_type=jnp.float32

time: 2130 us -> 2070 us (0.972)
  waiting for transfers between devices: 1310 us -> 1230 us
    ppermute x0 -> x12, waiting for transfers between devices: none -> 115 us  [grow_blocks(): lax.ppermute(blocks, axis, [(i, i ^ bit) for i in range(size)])]
    all_gather x3 -> x0, waiting for transfers between devices: 109 us -> none  [layer_forward(): lax.all_gather(keyval_local, ('dp', 'tensor'), axis=1, tiled=True)]
    all_gather x6, waiting for transfers between devices: 110 us -> 61.3 us  [spread_rows(): return lax.all_gather(values, 'tensor', axis=1, tiled=True)]
    all_gather x1, waiting for transfers between devices: 48.8 us -> 16.2 us  [local(): lax.all_gather(w_query, 'dp', axis=1, tiled=True)]
  transfers between devices with their start and end apart: 45 -> 54, of which waited for: 41 -> 47; matrix products, arithmetic and copies ran while one was open for 17% -> 18% of each run, Pallas kernels for 0% -> 0%
where the time goes in v1:
time: 2070 us; the launch traced here: 2060 us
  waiting for transfers between devices  1230 us (59%)
  matrix products  505 us (24%)
  other arithmetic  186 us (9%)
  local copies, waits for them, and re-layouts  46.5 us (2%)
  starting transfers between devices  39.4 us (2%)
  blocking collectives  34.1 us (2%)
    reduce_scatter x1, waiting for transfers between devices, local(): lax.psum_scatter(totals[3].astype(jnp.bfloat16), 'dp', scatter_dimension=...  167 us
    reduce_scatter x1, waiting for transfers between devices, local(): lax.psum_scatter(totals[2].astype(jnp.bfloat16), 'dp', scatter_dimension=...  165 us
    all_gather x1, waiting for transfers between devices, local(): lax.all_gather(w_hidden, 'dp', axis=1, tiled=True)  153 us
    all_gather x1, waiting for transfers between devices, local(): lax.all_gather(w_project, 'dp', axis=2, tiled=True)  139 us
    ppermute x12, waiting for transfers between devices, grow_blocks(): lax.ppermute(blocks, axis, [(i, i ^ bit) for i in range(size)])  115 us
    reduce_scatter x6, waiting for transfers between devices, collect_rows(): lax.psum_scatter(terms.astype(jnp.bfloat16), 'tensor', scatter_dimension=...  100 us
    all_gather x6, waiting for transfers between devices, spread_grads(): return lax.all_gather(values, 'tensor', axis=1, tiled=True)  69.5 us
    reduce_scatter x6, waiting for transfers between devices, collect_grads(): lax.psum_scatter(terms.astype(jnp.bfloat16), 'tensor', scatter_dimension=...  65.1 us
  transfers between devices with their start and end apart: 54, of which 47 were waited for; matrix products, arithmetic and copies ran while one was open for 18% of the time, Pallas kernels for 0%

profile of v1, /device:TPU:0, one launch (start us, length us, event | category | flops | bytes accessed | tf_op | source)
XLA Modules:
  0.0 2060.7 jit_solution(4006107390098840711)
XLA Ops:
  8.0 34.1 %all_gather.56 = bf16[1,4,2048]{2,1,0:T(4,128)(2,1)S(1)} all-gather(bf16[1,4,128]{2,1,0:T(4,128)(2,1)} %param.15), channel_id=1, replica_groups=mesh['section'=2,'dp'=8,'tensor'=2] {'dp','tensor'}, dimensions={2}, use_global_device_ids=true | all-gather | bytes 17408 | tf_op jit(solution)/shard_map/all_gather | solution.py:273
  74.1 37.2 %collective-permute-done.3 = bf16[8,1,128,256]{3,2,1,0:T(8,128)(2,1)} collective-permute-done((bf16[8,1,128,256]{3,2,1,0:T(8,128)(2,1)}, bf16[8,1,128,256]{3,2,1,0:T(8,128)(2,1)}, u32[]{:S(2)}, u32[]{:S(2)}) %collective-permute-start.3) | collective-permute-done | bytes 524320 | tf_op jit(solution)/shard_map/ppermute | solution.py:22
  157.5 19.6 all-gather.27.cloned.1.call-done
  181.5 18.6 reduce-scatter.21.cloned.1.call-done
  207.6 19.7 all-gather.29.cloned.1.call-done
  227.3 152.8 %all-gather.31.cloned.1.call-done = bf16[1,2048,4096]{2,1,0:T(8,128)(2,1)} async-done(((bf16[1,256,4096]{2,1,0:T(8,128)(2,1)}), bf16[1,2048,4096]{2,1,0:T(8,128)(2,1)}) %all-gather.31.cloned.1.call-update) | async-done | bytes 16777232 | tf_op jit(solution)/shard_map/all_gather | solution.py:268
  392.7 139.1 %all-gather.19.cloned.1.call-done = bf16[1,4096,2048]{2,1,0:T(8,128)(2,1)} async-done(((bf16[1,4096,256]{2,1,0:T(8,128)(2,1)}), bf16[1,4096,2048]{2,1,0:T(8,128)(2,1)}) %all-gather.19.cloned.1.call-update) | async-done | bytes 16777232 | tf_op jit(solution)/shard_map/all_gather | solution.py:269
  544.9 18.6 reduce-scatter.23.cloned.1.call-done
  602.2 21.3 %collective-permute-done.8 = bf16[8,1,128,256]{3,2,1,0:T(8,128)(2,1)} collective-permute-done((bf16[8,1,128,256]{3,2,1,0:T(8,128)(2,1)}, bf16[8,1,128,256]{3,2,1,0:T(8,128)(2,1)}, u32[]{:S(2)}, u32[]{:S(2)}) %collective-permute-start.8) | collective-permute-done | bytes 524320 | tf_op jit(solution)/shard_map/ppermute | solution.py:22
  659.6 21.2 %reduce-scatter.25.cloned.1.call-done = bf16[1,128,2048]{2,1,0:T(8,128)(2,1)} async-done(((bf16[1,256,2048]{2,1,0:T(8,128)(2,1)}), bf16[1,128,2048]{2,1,0:T(8,128)(2,1)}) %reduce-scatter.25.cloned.1.call-update) | async-done | bytes 524304 | tf_op jit(solution)/shard_map/reduce_scatter | solution.py:68
  686.6 21.4 %all-gather.35.cloned.1.call-done = bf16[1,256,2048]{2,1,0:T(8,128)(2,1)} async-done(((bf16[1,128,2048]{2,1,0:T(8,128)(2,1)}), bf16[1,256,2048]{2,1,0:T(8,128)(2,1)}) %all-gather.35.cloned.1.call-update) | async-done | bytes 1048592 | tf_op jit(solution)/shard_map/all_gather | solution.py:64
  730.2 20.4 reduce-scatter.27.cloned.1.call-done
  787.4 22.2 %collective-permute-done.13 = bf16[8,1,128,256]{3,2,1,0:T(8,128)(2,1)} collective-permute-done((bf16[8,1,128,256]{3,2,1,0:T(8,128)(2,1)}, bf16[8,1,128,256]{3,2,1,0:T(8,128)(2,1)}, u32[]{:S(2)}, u32[]{:S(2)}) %collective-permute-start.13) | collective-permute-done | bytes 524320 | tf_op jit(solution)/shard_map/ppermute | solution.py:22
  842.3 21.4 %reduce-scatter.29.cloned.1.call-done = bf16[1,128,2048]{2,1,0:T(8,128)(2,1)} async-done(((bf16[1,256,2048]{2,1,0:T(8,128)(2,1)}), bf16[1,128,2048]{2,1,0:T(8,128)(2,1)}) %reduce-scatter.29.cloned.1.call-update) | async-done | bytes 524304 | tf_op jit(solution)/shard_map/reduce_scatter | solution.py:68
  870.8 20.1 all-gather.39.cloned.1.call-done
  1094.0 20.7 %all-gather.43.cloned.1.call-done = bf16[1,256,2048]{2,1,0:T(8,128)(2,1)} async-done(((bf16[1,128,2048]{2,1,0:T(8,128)(2,1)}), bf16[1,256,2048]{2,1,0:T(8,128)(2,1)}) %all-gather.43.cloned.1.call-update) | async-done | bytes 1048592 | tf_op jit(solution)/shard_map/all_gather | solution.py:74
  1139.1 20.6 reduce-scatter.35.cloned.1.call-done
  1246.6 19.1 all-to-all-done.1
  1296.1 20.7 %all-gather.47.cloned.1.call-done = bf16[1,256,2048]{2,1,0:T(8,128)(2,1)} async-done(((bf16[1,128,2048]{2,1,0:T(8,128)(2,1)}), bf16[1,256,2048]{2,1,0:T(8,128)(2,1)}) %all-gather.47.cloned.1.call-update) | async-done | bytes 1048592 | tf_op jit(solution)/shard_map/all_gather | solution.py:74
  1542.0 30.4 %fusion.1 = bf16[1,4096,2048]{2,1,0:T(8,128)(2,1)} fusion(f32[4096,2048]{1,0:T(8,128)} %fusion.230, f32[4096,2048]{1,0:T(8,128)} %fusion.232, f32[]{:T(128)S(6)} %convert_element_type.640, f32[]{:T(128)S(6)} %convert_element_type.639, f32[]{:T(128)S(6)} %convert_element_type.638, bf16[3,1,256,4096]{3,2,1,0:T(8,128)(2,1)} %copy-done.12, s32[]{:T(128)S(6)} %min.35, ...), kind=kOutput, calls=%fused_computation.3 | convolution fusion | flops 4345298944 | bytes 87031824 | tf_op jit(solution)/shard_map/sqf,sqd->fd/dot_general | solution.py:249
  1602.1 30.1 %fusion = bf16[1,2048,4096]{2,1,0:T(8,128)(2,1)} fusion(f32[2048,4096]{1,0:T(8,128)} %fusion.358, f32[2048,4096]{1,0:T(8,128)} %fusion.360, f32[]{:T(128)S(6)} %convert_element_type.640, f32[]{:T(128)S(6)} %convert_element_type.639, f32[]{:T(128)S(6)} %convert_element_type.638, bf16[256,4096]{1,0:T(8,128)(2,1)} %fusion.88, ...), kind=kOutput, calls=%fused_computation.2 | convolution fusion | flops 4345298944 | bytes 87031824 | tf_op jit(solution)/shard_map/sqd,sqf->df/dot_general | solution.py:246
  1653.5 166.6 %reduce-scatter.53.cloned.1.call-done = bf16[1,4096,256]{2,1,0:T(8,128)(2,1)} async-done(((bf16[1,4096,2048]{2,1,0:T(8,128)(2,1)}), bf16[1,4096,256]{2,1,0:T(8,128)(2,1)}) %reduce-scatter.53.cloned.1.call-update) | async-done | bytes 2097168 | tf_op jit(solution)/shard_map/reduce_scatter | solution.py:347
  1824.1 165.2 %reduce-scatter.51.cloned.1.call-done = bf16[1,256,4096]{2,1,0:T(8,128)(2,1)} async-done(((bf16[1,2048,4096]{2,1,0:T(8,128)(2,1)}), bf16[1,256,4096]{2,1,0:T(8,128)(2,1)}) %reduce-scatter.51.cloned.1.call-update) | async-done | bytes 2097168 | tf_op jit(solution)/shard_map/reduce_scatter | solution.py:344
  1993.4 60.6 %reduce-scatter.47.cloned.1.call-done = f32[1,128,256]{2,1,0:T(8,128)} async-done(((f32[1,2048,256]{2,1,0:T(8,128)}), f32[1,128,256]{2,1,0:T(8,128)}) %reduce-scatter.47.cloned.1.call-update) | async-done | bytes 131088 | tf_op jit(solution)/shard_map/reduce_scatter | solution.py:352
  (688 shorter events, 921.6 us)
Async XLA Ops:
  7.9 104.7 %all-gather.23.cloned.1.call-start = ((), (), s32[]{:S(2)}) async-start(), calls=%async_computation.23 | async-start | bytes 1572864 | tf_op jit(solution)/shard_map/all_gather | solution.py:64
  44.9 83.9 %all-gather.25.cloned.1.call-start = ((), (), s32[]{:S(2)}) async-start(), calls=%async_computation.24 | async-start | bytes 4718592 | tf_op jit(solution)/shard_map/all_gather | solution.py:266
  45.7 131.4 %all-gather.27.cloned.1.call-start = ((), (), s32[]{:S(2)}) async-start(), calls=%async_computation.25 | async-start | bytes 4718592 | tf_op jit(solution)/shard_map/all_gather | solution.py:267
  46.2 153.9 %reduce-scatter.21.cloned.1.call-start = ((), (), s32[]{:S(2)}) async-start(), calls=%async_computation.26 | async-start | bytes 1572864 | tf_op jit(solution)/shard_map/reduce_scatter | solution.py:68
  205.8 174.3 %all-gather.31.cloned.1.call-start = ((), (), s32[]{:S(2)}) async-start(), calls=%async_computation.28 | async-start | bytes 18874368 | tf_op jit(solution)/shard_map/all_gather | solution.py:268
  206.6 325.3 %all-gather.19.cloned.1.call-start = ((), (), s32[]{:S(2)}) async-start(), calls=%async_computation.21 | async-start | bytes 18874368 | tf_op jit(solution)/shard_map/all_gather | solution.py:269
  207.3 356.1 %reduce-scatter.23.cloned.1.call-start = ((), (), s32[]{:S(2)}) async-start(), calls=%async_computation.29 | async-start | bytes 1572864 | tf_op jit(solution)/shard_map/reduce_scatter | solution.py:68
  544.8 80.9 %all-gather.33.cloned.1.call-start = ((), (), s32[]{:S(2)}) async-start(), calls=%async_computation.30 | async-start | bytes 1572864 | tf_op jit(solution)/shard_map/all_gather | solution.py:64
  588.7 92.1 %reduce-scatter.25.cloned.1.call-start = ((), (), s32[]{:S(2)}) async-start(), calls=%async_computation.31 | async-start | bytes 1572864 | tf_op jit(solution)/shard_map/reduce_scatter | solution.py:68
  730.1 80.7 %all-gather.37.cloned.1.call-start = ((), (), s32[]{:S(2)}) async-start(), calls=%async_computation.34 | async-start | bytes 1572864 | tf_op jit(solution)/shard_map/all_gather | solution.py:64
  775.2 88.5 %reduce-scatter.29.cloned.1.call-start = ((), (), s32[]{:S(2)}) async-start(), calls=%async_computation.35 | async-start | bytes 1572864 | tf_op jit(solution)/shard_map/reduce_scatter | solution.py:68
  870.3 87.9 %reduce-scatter.31.cloned.1.call-start = ((), (), s32[]{:S(2)}) async-start(), calls=%async_computation.37 | async-start | bytes 1572864 | tf_op jit(solution)/shard_map/reduce_scatter | solution.py:78
  1045.1 69.6 %all-gather.43.cloned.1.call-start = ((), (), s32[]{:S(2)}) async-start(), calls=%async_computation.40 | async-start | bytes 1572864 | tf_op jit(solution)/shard_map/all_gather | solution.py:74
  1093.9 65.8 %reduce-scatter.35.cloned.1.call-start = ((), (), s32[]{:S(2)}) async-start(), calls=%async_computation.41 | async-start | bytes 1572864 | tf_op jit(solution)/shard_map/reduce_scatter | solution.py:78
  1246.5 70.3 %all-gather.47.cloned.1.call-start = ((), (), s32[]{:S(2)}) async-start(), calls=%async_computation.44 | async-start | bytes 1572864 | tf_op jit(solution)/shard_map/all_gather | solution.py:74
  1296.0 65.6 %reduce-scatter.39.cloned.1.call-start = ((), (), s32[]{:S(2)}) async-start(), calls=%async_computation.45 | async-start | bytes 1572864 | tf_op jit(solution)/shard_map/reduce_scatter | solution.py:78
  1367.3 109.0 %reduce-scatter.41.cloned.1.call-start = ((), (), s32[]{:S(2)}) async-start(), calls=%async_computation.47 | async-start | bytes 1572864 | tf_op jit(solution)/shard_map/reduce_scatter | solution.py:78
  1451.1 186.2 %reduce-scatter.43.cloned.1.call-start = ((), (), s32[]{:S(2)}) async-start(), calls=%async_computation.48 | async-start | bytes 1572864 | tf_op jit(solution)/shard_map/reduce_scatter | solution.py:68
  1464.3 176.8 %reduce-scatter.55.cloned.1.call-start = ((), (), s32[]{:S(2)}) async-start(), calls=%async_computation.55 | async-start | bytes 1114112
  1488.6 154.8 %reduce-scatter.49.cloned.1.call-start = ((), (), s32[]{:S(2)}) async-start(), calls=%async_computation.51 | async-start | bytes 4718592 | tf_op jit(solution)/shard_map/reduce_scatter | solution.py:341
  1497.8 153.6 %reduce-scatter.45.cloned.1.call-start = ((), (), s32[]{:S(2)}) async-start(), calls=%async_computation.49 | async-start | bytes 4718592 | tf_op jit(solution)/shard_map/reduce_scatter | solution.py:338
  1509.3 310.8 %reduce-scatter.53.cloned.1.call-start = ((), (), s32[]{:S(2)}) async-start(), calls=%async_computation.53 | async-start | bytes 18874368 | tf_op jit(solution)/shard_map/reduce_scatter | solution.py:347
  1572.4 416.8 %reduce-scatter.51.cloned.1.call-start = ((), (), s32[]{:S(2)}) async-start(), calls=%async_computation.52 | async-start | bytes 18874368 | tf_op jit(solution)/shard_map/reduce_scatter | solution.py:344
  1632.3 421.7 %reduce-scatter.47.cloned.1.call-start = ((), (), s32[]{:S(2)}) async-start(), calls=%async_computation.50 | async-start | bytes 2228224 | tf_op jit(solution)/shard_map/reduce_scatter | solution.py:352
  (193 other events, 5885.7 us)
Sparse Core Ops, SparseCore 0:
  10.2 40.6 all-gather.20
  75.0 53.7 all-gather.24
  130.2 46.7 all-gather.26
  205.9 21.3 all-gather.28
  229.0 151.0 all-gather.30
  381.8 150.0 all-gather.18
  588.8 21.3 all-gather.32
  659.5 21.2 reduce-scatter.24
  686.6 21.3 all-gather.34
  775.3 21.3 all-gather.36
  869.5 21.3 all-gather.38
  892.3 21.2 all-gather.50
  964.1 21.3 all-gather.40
  1045.2 27.5 reduce-scatter.32
  1165.7 21.2 all-gather.44
  1246.7 27.5 reduce-scatter.36
  1367.4 21.3 all-gather.48
  1464.4 23.4 reduce-scatter.42
  1491.5 57.3 reduce-scatter.54
  1551.2 48.9 reduce-scatter.48
  1603.2 48.1 reduce-scatter.44
  1653.7 166.3 reduce-scatter.52
  1822.6 166.6 reduce-scatter.50
  1994.0 59.9 reduce-scatter.46
  (11 shorter events, 221.0 us)
